TPU v7x, 32 devices: a whole 2x2x4 slice. The times are simulated.
32 devices in a mesh: dp: 8 (over z, x), cluster: 4 (over y, core).
Axes of the slice: x: 2, y: 2, z: 4, core: 2. Of those that a mesh axis runs over, the one named last changes fastest.
Arguments:
- home_rows: bfloat16 [49152, 768], P(('dp', 'cluster')), may hold values from -6 to 6
- guest_rows: bfloat16 [8192, 768], P(('dp', 'cluster')), may hold values from -6 to 6
- home_cluster: int32 [192], replicated, may hold values from 0 to 7, as said below
- guest_cluster: int32 [32], replicated, may hold values from 0 to 7, as said below
- pair_mask: int32 [32, 6, 8], P(('dp', 'cluster')), may hold values from 0 to 1, as said below
Outputs:
- home_score: float32 [49152], P(('dp', 'cluster'))
- guest_score: float32 [8192], P(('dp', 'cluster'))
Inputs may be any that keep to these rules, and one draw needn't show every extreme that they name: `home_cluster`: blocks of the devices at cluster indices 2 g and 2 g + 1 carry ids from g * 4 to (g + 1) * 4 - 1. `guest_cluster`: blocks of the devices at cluster indices 2 g and 2 g + 1 carry ids from g * 4 to (g + 1) * 4 - 1. `pair_mask`: an entry is 1 where the resident block and the visiting block it names carry one cluster id, else 0.
All inputs are finite; a program needn't handle non-finite values.
Results may differ from a plain program's by a relative error of at most 0.0003.
Values may be sent and summed in bfloat16 or wider, within the bound.
A program may use at most 128 MiB of HBM per device.

v0:
```python
import jax
import jax.numpy as jnp
from jax import lax
from jax.sharding import PartitionSpec as P

BLOCK = 256


SHARPNESS = 30.0
EPSILON = 1e-06


def swapped(value, axis, apart):
    mask = 2**apart
    pairs = [(source, source ^ mask) for source in range(lax.axis_size(axis))]
    return lax.ppermute(value, axis, pairs)


def passed_along(block, axis, distance):
    devices = range(lax.axis_size(axis))
    route = [((i - distance) % len(devices), i) for i in devices]
    return lax.ppermute(block, axis, route)


def inverse_norms(rows):
    values = rows.astype(jnp.float32)
    return 1.0 / jnp.sqrt(jnp.sum(values * values, axis=-1) + EPSILON)


def body(home_rows, guest_rows, home_cluster, guest_cluster, pair_mask):
    slots = home_rows.shape[0] // BLOCK
    ndp_size = lax.axis_size("dp")
    resident = home_rows.reshape(slots, BLOCK, home_rows.shape[1])
    inv_resident = inverse_norms(resident)
    listed_mask = pair_mask[0]
    position = lax.axis_index("dp")

    def visit(state_pair, visitor, anchor):
        row_acc, col_parts = state_pair
        inv_visitor = inverse_norms(visitor)
        listed = lax.dynamic_slice_in_dim(listed_mask, anchor, 1, 1)[:, 0]
        col_total = jnp.zeros((BLOCK,), jnp.float32)
        row_pieces = []
        for slot in range(slots):

            def compute(operand):
                products = jnp.einsum(
                    "rd,cd->rc", resident[slot], visitor, preferred_element_type=jnp.float32
                )
                kernel_tile = jnp.exp(
                    SHARPNESS * (products * inv_resident[slot][:, None] * inv_visitor[None, :])
                )
                return (jnp.sum(kernel_tile, axis=1), jnp.sum(kernel_tile, axis=0))

            def passing(operand):
                return (jnp.zeros((BLOCK,), jnp.float32), jnp.zeros((BLOCK,), jnp.float32))

            row_part, col_part = lax.cond(listed[slot] > 0, compute, passing, 0)
            row_pieces.append(row_part)
            col_total = col_total + col_part
        row_acc = row_acc + jnp.stack(row_pieces)
        col_parts = lax.dynamic_update_slice_in_dim(col_parts, col_total[None, :], anchor, 0)
        return (row_acc, col_parts)

    start_pair = (jnp.zeros((slots, BLOCK), jnp.float32), jnp.zeros((ndp_size, BLOCK), jnp.float32))
    arrived = swapped(guest_rows, "cluster", 0)
    first_pair = visit(start_pair, arrived, position)

    def turn_single(step, carried):
        state_pair, visitor = carried
        visitor = passed_along(visitor, "dp", 1)
        anchor = (position - step) % ndp_size
        return (visit(state_pair, visitor, anchor), visitor)

    final_pair, last_visitor = lax.fori_loop(1, ndp_size, turn_single, (first_pair, arrived))
    row_acc, col_parts = final_pair
    col_home = lax.psum_scatter(col_parts, "dp", scatter_dimension=0, tiled=True)
    guest_density = swapped(col_home, "cluster", 0)[0]
    device = lax.axis_index(("dp", "cluster"))
    home_ids = lax.dynamic_slice_in_dim(home_cluster, device * slots, slots, 0)
    guest_id = lax.dynamic_slice_in_dim(guest_cluster, device, 1, 0)
    home_members = jnp.sum((home_cluster[None, :] == home_ids[:, None]).astype(jnp.int32), axis=1)
    home_members = home_members + jnp.sum(
        (guest_cluster[None, :] == home_ids[:, None]).astype(jnp.int32), axis=1
    )
    guest_members = jnp.sum((home_cluster[None, :] == guest_id[:, None]).astype(jnp.int32), axis=1)
    guest_members = guest_members + jnp.sum(
        (guest_cluster[None, :] == guest_id[:, None]).astype(jnp.int32), axis=1
    )
    home_score = jnp.log(1.0 + row_acc) - jnp.log(home_members.astype(jnp.float32))[:, None]
    guest_score = jnp.log(1.0 + guest_density) - jnp.log(guest_members.astype(jnp.float32))
    return (home_score.reshape(-1), guest_score)


def solution(mesh):
    placed = (
        P(("dp", "cluster"), None),
        P(("dp", "cluster"), None),
        P(),
        P(),
        P(("dp", "cluster"), None, None),
    )
    return jax.shard_map(
        body,
        mesh=mesh,
        in_specs=placed,
        out_specs=(P(("dp", "cluster")), P(("dp", "cluster"))),
        check_vma=False,
    )
```

profile of v0, /device:TPU:1, one launch (start us, length us, event | category | flops | bytes accessed | tf_op | source)
XLA Modules:
  0.0 134.3 jit_solution(14768264229732259476)
XLA Ops:
  0.8 2.3 %multiply_reduce_fusion.1 = f32[1536]{0:T(1024)S(1)} fusion(bf16[1536,768]{1,0:T(8,128)(2,1)} %param.31), kind=kLoop, calls=%fused_computation.76 | loop fusion | flops 3537408 | bytes 2365440 | tf_op jit(solution)/shard_map/reduce_sum | solution.py:27
  3.8 1.4 %fusion.60 = s32[]{:T(128)} fusion(s32[192]{0:T(256)S(1)} %copy-done.2, s32[]{:T(128)} %bitcast.51), kind=kLoop, calls=%fused_computation.91 | loop fusion | flops 575 | bytes 776 | tf_op jit(solution)/shard_map/reduce_sum | solution.py:86
  5.4 1.3 fusion.61
  6.7 0.7 constant_dynamic-slice_fusion.6
  12.4 0.7 dynamic-slice.1
  15.1 92.5 %while.19 = (s32[]{:T(128)}, f32[6,256]{1,0:T(8,128)S(1)}, f32[8,256]{1,0:T(8,128)S(1)}, bf16[256,768]{1,0:T(8,128)(2,1)S(1)}, s32[]{:T(128)}, /*index=5*/s32[6,...) while((s32[]{:T(128)}, f32[6,256]{1,0:T(8,128)S(1)}, ...), condition=%wide.region_52.53_spmd, body=%wide.region_26.52_spmd.sunk | while | flops 606535424 | bytes 7551612 | solution.py:75
  15.1 1.8 %collective-permute-start = (bf16[256,768]{1,0:T(8,128)(2,1)S(1)}, bf16[256,768]{1,0:T(8,128)(2,1)S(1)}, u32[]{:S(2)}, u32[]{:S(2)}) collective-permute-start(bf16[256,768]{1,0:T(8,128)(2,1)S(1)} %get-tuple-element.609), channel_id=1, source_target_pairs={{28,0},{0,4},{4,8},{8,12},{12,16},{16,20},{20,24},{24,28},{29,1},{... | collective-permute-start | bytes 1179656 | tf_op jit(solution)/shard_map/while/body/eval_jaxpr/ppermute | solution.py:22
  21.1 8.6 %collective-permute-done = bf16[256,768]{1,0:T(8,128)(2,1)S(1)} collective-permute-done((bf16[256,768]{1,0:T(8,128)(2,1)S(1)}, bf16[256,768]{1,0:T(8,128)(2,1)S(1)}, u32[]{:S(2)}, u32[]{:S(2)}) %collective-permute-start) | collective-permute-done | bytes 393248 | tf_op jit(solution)/shard_map/while/body/eval_jaxpr/ppermute | solution.py:22
  31.7 0.6 fusion.88
  35.9 8.9 %collective-permute-done = bf16[256,768]{1,0:T(8,128)(2,1)S(1)} collective-permute-done((bf16[256,768]{1,0:T(8,128)(2,1)S(1)}, bf16[256,768]{1,0:T(8,128)(2,1)S(1)}, u32[]{:S(2)}, u32[]{:S(2)}) %collective-permute-start) | collective-permute-done | bytes 393248 | tf_op jit(solution)/shard_map/while/body/eval_jaxpr/ppermute | solution.py:22
  45.9 0.6 fusion.88
  50.1 6.7 %collective-permute-done = bf16[256,768]{1,0:T(8,128)(2,1)S(1)} collective-permute-done((bf16[256,768]{1,0:T(8,128)(2,1)S(1)}, bf16[256,768]{1,0:T(8,128)(2,1)S(1)}, u32[]{:S(2)}, u32[]{:S(2)}) %collective-permute-start) | collective-permute-done | bytes 393248 | tf_op jit(solution)/shard_map/while/body/eval_jaxpr/ppermute | solution.py:22
  58.8 0.6 fusion.88
  63.1 7.0 %collective-permute-done = bf16[256,768]{1,0:T(8,128)(2,1)S(1)} collective-permute-done((bf16[256,768]{1,0:T(8,128)(2,1)S(1)}, bf16[256,768]{1,0:T(8,128)(2,1)S(1)}, u32[]{:S(2)}, u32[]{:S(2)}) %collective-permute-start) | collective-permute-done | bytes 393248 | tf_op jit(solution)/shard_map/while/body/eval_jaxpr/ppermute | solution.py:22
  72.1 0.6 fusion.88
  76.3 7.3 %collective-permute-done = bf16[256,768]{1,0:T(8,128)(2,1)S(1)} collective-permute-done((bf16[256,768]{1,0:T(8,128)(2,1)S(1)}, bf16[256,768]{1,0:T(8,128)(2,1)S(1)}, u32[]{:S(2)}, u32[]{:S(2)}) %collective-permute-start) | collective-permute-done | bytes 393248 | tf_op jit(solution)/shard_map/while/body/eval_jaxpr/ppermute | solution.py:22
  85.6 0.6 fusion.88
  89.8 6.0 %collective-permute-done = bf16[256,768]{1,0:T(8,128)(2,1)S(1)} collective-permute-done((bf16[256,768]{1,0:T(8,128)(2,1)S(1)}, bf16[256,768]{1,0:T(8,128)(2,1)S(1)}, u32[]{:S(2)}, u32[]{:S(2)}) %collective-permute-start) | collective-permute-done | bytes 393248 | tf_op jit(solution)/shard_map/while/body/eval_jaxpr/ppermute | solution.py:22
  97.4 0.6 fusion.88
  101.6 5.0 %collective-permute-done = bf16[256,768]{1,0:T(8,128)(2,1)S(1)} collective-permute-done((bf16[256,768]{1,0:T(8,128)(2,1)S(1)}, bf16[256,768]{1,0:T(8,128)(2,1)S(1)}, u32[]{:S(2)}, u32[]{:S(2)}) %collective-permute-start) | collective-permute-done | bytes 393248 | tf_op jit(solution)/shard_map/while/body/eval_jaxpr/ppermute | solution.py:22
  107.6 13.9 %all-reduce = f32[8,256]{1,0:T(8,128)S(1)} all-reduce(f32[8,256]{1,0:T(8,128)S(1)} %get-tuple-element.407), channel_id=2, replica_groups=mesh['dp'=8,'cluster'=4] {'dp'}, use_global_device_ids=true, to_apply=%region_55.56.clone | all-reduce | flops 2048 | bytes 16384
  121.5 0.7 constant_dynamic-slice_fusion.7
  122.2 10.7 %collective-permute-start.2 = (f32[1,256]{1,0:T(1,128)S(1)}, f32[1,256]{1,0:T(1,128)S(1)}, u32[]{:S(2)}, u32[]{:S(2)}) collective-permute-start(f32[1,256]{1,0:T(1,128)S(1)} %constant_dynamic-slice_fusion.7), channel_id=1, source_target_pairs={{0,1},{1,0},{2,3},{3,2},{4,5},{5,4},{6,7},{7,6},{8,9},{9,8},{10,11... | collective-permute-start | bytes 3080 | tf_op jit(solution)/shard_map/ppermute | solution.py:16
  133.0 0.6 reshape.142
  (236 shorter events, 23.5 us)
Async XLA Ops:
  0.6 11.8 %copy-start.4 = (u32[32]{0:T(128)S(1)}, u32[32]{0:T(128)}, u32[]{:S(2)}) copy-start(u32[32]{0:T(128)} %constant.189) | copy-start | bytes 388
  0.6 12.8 %copy-start = (bf16[1536,768]{1,0:T(8,128)(2,1)S(1)}, bf16[1536,768]{1,0:T(8,128)(2,1)}, u32[]{:S(2)}) copy-start(bf16[1536,768]{1,0:T(8,128)(2,1)} %param.31) | copy-start | bytes 7077892
  0.7 2.5 %copy-start.3 = (s32[32]{0:T(128)S(1)}, s32[32]{0:T(128)}, u32[]{:S(2)}) copy-start(s32[32]{0:T(128)} %param.34) | copy-start | bytes 388
  0.7 3.1 %copy-start.2 = (s32[192]{0:T(256)S(1)}, s32[192]{0:T(256)}, u32[]{:S(2)}) copy-start(s32[192]{0:T(256)} %param.33) | copy-start | bytes 2308
  0.7 6.0 %copy-start.1 = (s32[1,6,8]{2,0,1:T(1,128)S(1)}, s32[1,6,8]{2,0,1:T(1,128)}, u32[]{:S(2)}) copy-start(s32[1,6,8]{2,0,1:T(1,128)} %param.35) | copy-start | bytes 580
  0.7 12.6 %collective-permute-start.1 = (bf16[256,768]{1,0:T(8,128)(2,1)}, bf16[256,768]{1,0:T(8,128)(2,1)S(1)}, u32[]{:S(2)}, u32[]{:S(2)}) collective-permute-start(bf16[256,768]{1,0:T(8,128)(2,1)} %param.32), channel_id=1, source_target_pairs={{0,1},{1,0},{2,3},{3,2},{4,5},{5,4},{6,7},{7,6},{8,9},{9,8},{10,11... | collective-permute-start | bytes 1179656 | tf_op jit(solution)/shard_map/ppermute | solution.py:16
  15.1 14.6 %collective-permute-start = (bf16[256,768]{1,0:T(8,128)(2,1)S(1)}, bf16[256,768]{1,0:T(8,128)(2,1)S(1)}, u32[]{:S(2)}, u32[]{:S(2)}) collective-permute-start(bf16[256,768]{1,0:T(8,128)(2,1)S(1)} %get-tuple-element.609), channel_id=1, source_target_pairs={{28,0},{0,4},{4,8},{8,12},{12,16},{16,20},{20,24},{24,28},{29,1},{... | collective-permute-start | bytes 1179656 | tf_op jit(solution)/shard_map/while/body/eval_jaxpr/ppermute | solution.py:22
  31.5 13.3 %collective-permute-start = (bf16[256,768]{1,0:T(8,128)(2,1)S(1)}, bf16[256,768]{1,0:T(8,128)(2,1)S(1)}, u32[]{:S(2)}, u32[]{:S(2)}) collective-permute-start(bf16[256,768]{1,0:T(8,128)(2,1)S(1)} %get-tuple-element.609), channel_id=1, source_target_pairs={{28,0},{0,4},{4,8},{8,12},{12,16},{16,20},{20,24},{24,28},{29,1},{... | collective-permute-start | bytes 1179656 | tf_op jit(solution)/shard_map/while/body/eval_jaxpr/ppermute | solution.py:22
  45.8 11.1 %collective-permute-start = (bf16[256,768]{1,0:T(8,128)(2,1)S(1)}, bf16[256,768]{1,0:T(8,128)(2,1)S(1)}, u32[]{:S(2)}, u32[]{:S(2)}) collective-permute-start(bf16[256,768]{1,0:T(8,128)(2,1)S(1)} %get-tuple-element.609), channel_id=1, source_target_pairs={{28,0},{0,4},{4,8},{8,12},{12,16},{16,20},{20,24},{24,28},{29,1},{... | collective-permute-start | bytes 1179656 | tf_op jit(solution)/shard_map/while/body/eval_jaxpr/ppermute | solution.py:22
  58.7 11.4 %collective-permute-start = (bf16[256,768]{1,0:T(8,128)(2,1)S(1)}, bf16[256,768]{1,0:T(8,128)(2,1)S(1)}, u32[]{:S(2)}, u32[]{:S(2)}) collective-permute-start(bf16[256,768]{1,0:T(8,128)(2,1)S(1)} %get-tuple-element.609), channel_id=1, source_target_pairs={{28,0},{0,4},{4,8},{8,12},{12,16},{16,20},{20,24},{24,28},{29,1},{... | collective-permute-start | bytes 1179656 | tf_op jit(solution)/shard_map/while/body/eval_jaxpr/ppermute | solution.py:22
  71.9 11.7 %collective-permute-start = (bf16[256,768]{1,0:T(8,128)(2,1)S(1)}, bf16[256,768]{1,0:T(8,128)(2,1)S(1)}, u32[]{:S(2)}, u32[]{:S(2)}) collective-permute-start(bf16[256,768]{1,0:T(8,128)(2,1)S(1)} %get-tuple-element.609), channel_id=1, source_target_pairs={{28,0},{0,4},{4,8},{8,12},{12,16},{16,20},{20,24},{24,28},{29,1},{... | collective-permute-start | bytes 1179656 | tf_op jit(solution)/shard_map/while/body/eval_jaxpr/ppermute | solution.py:22
  85.4 10.4 %collective-permute-start = (bf16[256,768]{1,0:T(8,128)(2,1)S(1)}, bf16[256,768]{1,0:T(8,128)(2,1)S(1)}, u32[]{:S(2)}, u32[]{:S(2)}) collective-permute-start(bf16[256,768]{1,0:T(8,128)(2,1)S(1)} %get-tuple-element.609), channel_id=1, source_target_pairs={{28,0},{0,4},{4,8},{8,12},{12,16},{16,20},{20,24},{24,28},{29,1},{... | collective-permute-start | bytes 1179656 | tf_op jit(solution)/shard_map/while/body/eval_jaxpr/ppermute | solution.py:22
  97.2 9.4 %collective-permute-start = (bf16[256,768]{1,0:T(8,128)(2,1)S(1)}, bf16[256,768]{1,0:T(8,128)(2,1)S(1)}, u32[]{:S(2)}, u32[]{:S(2)}) collective-permute-start(bf16[256,768]{1,0:T(8,128)(2,1)S(1)} %get-tuple-element.609), channel_id=1, source_target_pairs={{28,0},{0,4},{4,8},{8,12},{12,16},{16,20},{20,24},{24,28},{29,1},{... | collective-permute-start | bytes 1179656 | tf_op jit(solution)/shard_map/while/body/eval_jaxpr/ppermute | solution.py:22
  122.2 11.5 %collective-permute-start.2 = (f32[1,256]{1,0:T(1,128)S(1)}, f32[1,256]{1,0:T(1,128)S(1)}, u32[]{:S(2)}, u32[]{:S(2)}) collective-permute-start(f32[1,256]{1,0:T(1,128)S(1)} %constant_dynamic-slice_fusion.7), channel_id=1, source_target_pairs={{0,1},{1,0},{2,3},{3,2},{4,5},{5,4},{6,7},{7,6},{8,9},{9,8},{10,11... | collective-permute-start | bytes 3080 | tf_op jit(solution)/shard_map/ppermute | solution.py:16
where the time goes:
time: 135 us; the launch traced here: 134 us
  waiting for transfers between devices  49.6 us (37%)
  loops' own time  27.6 us (20%)
  blocking collectives  13.9 us (10%)
  starting transfers between devices  12.9 us (10%)
  local copies, waits for them, and re-layouts  9.01 us (7%)
  matrix products  7.98 us (6%)
  other arithmetic  7.4 us (5%)
  between operations  5.87 us (4%)
    ppermute x7, waiting for transfers between devices, passed_along(): return lax.ppermute(block, axis, route)  49.5 us
    another operation x1, loops' own time, body(): lax.fori_loop(1, ndp_size, turn_single, (first_pair, arrived))  26.1 us
    unnamed x1, blocking collectives  13.9 us
    ppermute x2, starting transfers between devices, swapped(): return lax.ppermute(value, axis, pairs)  10.8 us
    dot_general x19, matrix products, compute(): jnp.einsum('rd,cd->rc', resident[slot], visitor, preferred_element_type=j...  7.98 us
    slice x8, local copies, waits for them, and re-layouts, visit(): row_part, col_part = lax.cond(listed[slot] > 0, compute, passing, 0)  4.87 us
    reduce_sum x9, other arithmetic, inverse_norms(): return 1.0 / jnp.sqrt(jnp.sum(values * values, axis=-1) + EPSILON)  3.58 us
  transfers between devices with their start and end apart: 9, of which 8 were waited for; matrix products, arithmetic and copies ran while one was open for 9% of the time, Pallas kernels for 0%

commit v1 on v0

v1 whole, which is shorter than its diff:
```python
import functools

import jax
import jax.numpy as jnp
from jax import lax
from jax.experimental import pallas as pl
from jax.experimental.pallas import tpu as pltpu
from jax.sharding import PartitionSpec as P

BLOCK = 256
PARTS = 2
CHUNK = BLOCK // PARTS

SHARPNESS = 30.0
LOG2_E = 1.4426950408889634
EPSILON = 1e-06
MESH = pl.DeviceIdType.MESH


def lane_fold(value):
    return jnp.sum(value.reshape(value.shape[0] // 8, 8, value.shape[1]), axis=0)


def kernel(
    ndp, slots, home_ref, guest_ref, home_ids, guest_ids, mask_ref, home_out, guest_out,
    rows, turned, blocks, inv_home, home_acc, col_parts, inbox,
    load_sem, own_sem, line_sem, side_sem, recv_sem, col_send, col_recv,
):
    d = lax.axis_index("dp")
    c = lax.axis_index("cluster")
    n_cluster = lax.axis_size("cluster")
    count = ndp // 2
    z = lax.div(d, 2)
    x = lax.rem(d, 2)
    mirror = c + 1 - 2 * lax.rem(c, 2)
    beside = d + 1 - 2 * x
    has_up = z < count - 1
    has_down = z > 0

    load = pltpu.make_async_copy(home_ref, rows, load_sem)
    load.start()

    barrier = pltpu.get_barrier_semaphore()

    def greet(dp, cluster):
        pl.semaphore_signal(barrier, inc=1, device_id=(dp, cluster), device_id_type=MESH)

    greet(d, mirror)
    for column in (c, mirror):
        greet(beside, column)

        @pl.when(has_up)
        def _():
            greet(d + 2, column)

        @pl.when(has_down)
        def _():
            greet(d - 2, column)

    pl.semaphore_wait(barrier, 3 + 2 * has_up.astype(jnp.int32) + 2 * has_down.astype(jnp.int32))

    def own_copy(part, way, target):
        return pltpu.make_async_remote_copy(
            src_ref=guest_ref.at[pl.ds(part * CHUNK, CHUNK), :],
            dst_ref=blocks.at[d, part],
            send_sem=own_sem.at[way, part],
            recv_sem=recv_sem.at[d, part],
            device_id=(target, mirror),
            device_id_type=MESH,
        )

    def own_each(act):
        for part in range(PARTS):

            @pl.when(has_up)
            def _():
                act(own_copy(part, 0, d + 2))

            @pl.when(has_down)
            def _():
                act(own_copy(part, 1, d - 2))

            act(own_copy(part, 2, beside))
            act(own_copy(part, 3, d))

    own_each(lambda copy: copy.start())

    def passed(slot, part, sem, target):
        return pltpu.make_async_remote_copy(
            src_ref=blocks.at[slot, part],
            dst_ref=blocks.at[slot, part],
            send_sem=sem.at[slot, part],
            recv_sem=recv_sem.at[slot, part],
            device_id=(target, c),
            device_id_type=MESH,
        )

    def pass_each(zz, xx, part, act):
        slot = zz * 2 + xx
        on_line = xx == x
        last = part == PARTS - 1
        low = jnp.logical_and(last, zz == 0)
        high = jnp.logical_and(last, zz == count - 1)
        off_line = jnp.logical_not(on_line)
        go_up = jnp.logical_or(
            jnp.logical_and(on_line, zz < z), jnp.logical_and(off_line, low)
        )
        go_down = jnp.logical_or(
            jnp.logical_and(on_line, zz > z), jnp.logical_and(off_line, high)
        )
        go_side = jnp.logical_and(
            jnp.logical_and(on_line, zz != z), jnp.logical_not(jnp.logical_or(low, high))
        )

        @pl.when(jnp.logical_and(has_up, go_up))
        def _():
            act(passed(slot, part, line_sem, d + 2))

        @pl.when(jnp.logical_and(has_down, go_down))
        def _():
            act(passed(slot, part, line_sem, d - 2))

        @pl.when(go_side)
        def _():
            act(passed(slot, part, side_sem, beside))

    def col_copy(slot):
        return pltpu.make_async_remote_copy(
            src_ref=col_parts.at[slot],
            dst_ref=inbox.at[d],
            send_sem=col_send.at[slot],
            recv_sem=col_recv.at[d],
            device_id=(slot, mirror),
            device_id_type=MESH,
        )

    load.wait()

    def prepare(slot, carry):
        own = rows[pl.ds(pl.multiple_of(slot * BLOCK, BLOCK), BLOCK), :]
        flipped = own.T
        turned[slot] = flipped
        values = flipped.astype(jnp.float32)
        total = jnp.sum(lane_fold(values * values), axis=0, keepdims=True)
        scale = (SHARPNESS * LOG2_E) / jnp.sqrt(total + EPSILON)
        inv_home[slot] = jnp.broadcast_to(scale, (8, BLOCK))
        home_acc[slot] = jnp.zeros((8, BLOCK), jnp.float32)
        return carry

    lax.fori_loop(0, slots, prepare, 0)

    device = d * n_cluster + c
    wanted = [home_ids[device * slots + s] for s in range(slots)] + [guest_ids[device]]

    def counted(ids):
        def step(i, totals):
            value = ids[i]
            return tuple(t + (value == w).astype(jnp.int32) for t, w in zip(totals, wanted))

        return step

    members = tuple(jnp.int32(0) for _ in wanted)
    members = lax.fori_loop(0, home_ids.shape[0], counted(home_ids), members)
    members = lax.fori_loop(0, guest_ids.shape[0], counted(guest_ids), members)

    def compute(slot, part):
        visitor = blocks[slot, part]
        values = visitor.astype(jnp.float32)
        inv = 1.0 / jnp.sqrt(jnp.sum(values * values, axis=1, keepdims=True) + EPSILON)
        guest_acc = jnp.zeros((CHUNK, 128), jnp.float32)
        for s in range(slots):
            products = jnp.dot(visitor, turned[s], preferred_element_type=jnp.float32)
            tile = jnp.exp2(products * inv * inv_home[s, 0:1, :])
            listed = mask_ref[0, s, slot].astype(jnp.float32)
            home_acc[s] += lane_fold(tile) * listed
            guest_acc += (tile[:, :128] + tile[:, 128:]) * listed
        col_parts[slot, part] = lane_fold(guest_acc.T)

    def item(t, carry):
        k = lax.div(t, 4 * PARTS)
        r = lax.rem(t, 4 * PARTS)
        part = lax.div(r, 4)
        side = lax.div(lax.rem(r, 4), 2)
        plus = lax.rem(r, 2)
        dist = k - side
        zz = z + (2 * plus - 1) * dist
        xx = x + side * (1 - 2 * x)
        valid = (dist >= 0) & (dist < count) & (zz >= 0) & (zz < count)
        valid = valid & jnp.logical_not((dist == 0) & (plus == 1))

        @pl.when(valid)
        def _():
            slot = zz * 2 + xx
            passed(slot, part, line_sem, d).wait_recv()
            pass_each(zz, xx, part, lambda copy: copy.start())
            compute(slot, part)

            @pl.when(part == PARTS - 1)
            def _():
                col_copy(slot).start()

        return carry

    lax.fori_loop(0, (count + 1) * 4 * PARTS, item, 0)

    for s in range(slots):
        density = jnp.sum(home_acc[s], axis=0, keepdims=True)
        number = jnp.full((1, BLOCK), members[s], jnp.int32).astype(jnp.float32)
        home_out[s : s + 1, :] = jnp.log(1.0 + density) - jnp.log(number)

    own_each(lambda copy: copy.wait_send())

    def drain(t, carry):
        slot = lax.div(t, PARTS)
        part = lax.rem(t, PARTS)
        pass_each(lax.div(slot, 2), lax.rem(slot, 2), part, lambda copy: copy.wait_send())
        return carry

    lax.fori_loop(0, ndp * PARTS, drain, 0)

    def collect(t, total):
        pltpu.make_async_remote_copy(
            src_ref=col_parts.at[t],
            dst_ref=inbox.at[t],
            send_sem=col_send.at[t],
            recv_sem=col_recv.at[t],
            device_id=(t, mirror),
            device_id_type=MESH,
        ).wait_recv()
        return total + inbox[t]

    total = lax.fori_loop(0, ndp, collect, jnp.zeros((PARTS, 8, CHUNK), jnp.float32))
    number = jnp.full((1, CHUNK), members[slots], jnp.int32).astype(jnp.float32)
    for part in range(PARTS):
        density = jnp.sum(total[part], axis=0, keepdims=True)
        score = jnp.log(1.0 + density) - jnp.log(number)
        guest_out[:, part * CHUNK : (part + 1) * CHUNK] = score

    def col_drain(t, carry):
        col_copy(t).wait_send()
        return carry

    lax.fori_loop(0, ndp, col_drain, 0)


def body(home_rows, guest_rows, home_cluster, guest_cluster, pair_mask):
    slots = home_rows.shape[0] // BLOCK
    width = home_rows.shape[1]
    ndp = lax.axis_size("dp")
    hbm = pl.BlockSpec(memory_space=pl.ANY)
    smem = pl.BlockSpec(memory_space=pltpu.SMEM)
    vmem = pl.BlockSpec(memory_space=pltpu.VMEM)
    pairs = slots * ndp * BLOCK * BLOCK
    home_score, guest_score = pl.pallas_call(
        functools.partial(kernel, ndp, slots),
        out_shape=(
            jax.ShapeDtypeStruct((slots, BLOCK), jnp.float32),
            jax.ShapeDtypeStruct((1, BLOCK), jnp.float32),
        ),
        in_specs=[hbm, hbm, smem, smem, smem],
        out_specs=(vmem, vmem),
        scratch_shapes=[
            pltpu.VMEM((slots * BLOCK, width), jnp.bfloat16),
            pltpu.VMEM((slots, width, BLOCK), jnp.bfloat16),
            pltpu.VMEM((ndp, PARTS, CHUNK, width), jnp.bfloat16),
            pltpu.VMEM((slots, 8, BLOCK), jnp.float32),
            pltpu.VMEM((slots, 8, BLOCK), jnp.float32),
            pltpu.VMEM((ndp, PARTS, 8, CHUNK), jnp.float32),
            pltpu.VMEM((ndp, PARTS, 8, CHUNK), jnp.float32),
            pltpu.SemaphoreType.DMA,
            pltpu.SemaphoreType.DMA((4, PARTS)),
            pltpu.SemaphoreType.DMA((ndp, PARTS)),
            pltpu.SemaphoreType.DMA((ndp, PARTS)),
            pltpu.SemaphoreType.DMA((ndp, PARTS)),
            pltpu.SemaphoreType.DMA((ndp,)),
            pltpu.SemaphoreType.DMA((ndp,)),
        ],
        compiler_params=pltpu.CompilerParams(
            collective_id=0, has_side_effects=True, vmem_limit_bytes=48 * 2**20
        ),
        cost_estimate=pl.CostEstimate(
            flops=2 * pairs * width,
            bytes_accessed=2 * (home_rows.size + ndp * BLOCK * width),
            transcendentals=pairs,
        ),
    )(home_rows, guest_rows, home_cluster, guest_cluster, pair_mask)
    return (home_score.reshape(-1), guest_score.reshape(-1))


def solution(mesh):
    placed = (
        P(("dp", "cluster"), None),
        P(("dp", "cluster"), None),
        P(),
        P(),
        P(("dp", "cluster"), None, None),
    )
    return jax.shard_map(
        body,
        mesh=mesh,
        in_specs=placed,
        out_specs=(P(("dp", "cluster")), P(("dp", "cluster"))),
        check_vma=False,
    )
```

time: 135 us -> 50.9 us (0.38)
  waiting for transfers between devices: 49.6 us -> 0 us
  Pallas kernels: 0 us -> 44.2 us
  loops' own time: 27.6 us -> 0 us
  blocking collectives: 13.9 us -> 0 us
  starting transfers between devices: 12.9 us -> 0 us
  matrix products: 7.98 us -> 0 us
  other arithmetic: 7.4 us -> 0 us
  between operations: 5.87 us -> 0.64 us
  local copies, waits for them, and re-layouts: 9.01 us -> 5.84 us
    ppermute x9 -> x0, waiting for transfers between devices: 49.6 us -> none  [the longest x7 49.5 us: passed_along(): return lax.ppermute(block, axis, route)]
    pallas_call x0 -> x1, Pallas kernels: none -> 44.2 us  [body(): pl.pallas_call(functools.partial(kernel, ndp, slots), out_shape=(jax.Shap...]
    another operation x49 -> x0, loops' own time: 27.6 us -> none  [the longest x1 26.1 us: body(): lax.fori_loop(1, ndp_size, turn_single, (first_pair, arrived))]
    unnamed x1 -> x0, blocking collectives: 13.9 us -> none
    ppermute x9 -> x0, starting transfers between devices: 12.9 us -> none  [the longest x2 10.8 us: swapped(): return lax.ppermute(value, axis, pairs)]
    dot_general x19 -> x0, matrix products: 7.98 us -> none  [compute(): jnp.einsum('rd,cd->rc', resident[slot], visitor, preferred_element_type=j...]
    reduce_sum x13 -> x0, other arithmetic: 6.57 us -> none  [the longest x9 3.58 us: inverse_norms(): return 1.0 / jnp.sqrt(jnp.sum(values * values, axis=-1) + EPSILON)]
    slice x27 -> x0, local copies, waits for them, and re-layouts: 4.94 us -> none  [the longest x8 4.87 us: visit(): row_part, col_part = lax.cond(listed[slot] > 0, compute, passing, 0)]
  transfers between devices with their start and end apart: 9 -> 0, of which waited for: 8 -> 0; matrix products, arithmetic and copies ran while one was open for 9% -> 0% of each run, Pallas kernels for 0% -> 0%
where the time goes in v1:
time: 50.9 us; the launch traced here: 50.7 us
  Pallas kernels  44.2 us (87%)
  local copies, waits for them, and re-layouts  5.84 us (11%)
  between operations  0.64 us (1%)
    pallas_call x1, Pallas kernels, body(): pl.pallas_call(functools.partial(kernel, ndp, slots), out_shape=(jax.Shap...  44.2 us
    unnamed x10, local copies, waits for them, and re-layouts  5.24 us

profile of v1, /device:TPU:1, one launch (start us, length us, event | category | flops | bytes accessed | tf_op | source)
XLA Modules:
  0.0 50.7 jit_solution(3655975056468042015)
XLA Ops:
  0.6 0.7 %copy.7.mask_ref = s32[1,6,8]{2,1,0:T(8,128)S(1)} copy(s32[1,6,8]{2,0,1:T(1,128)} %param.9) | data formatting | bytes 384 | tf_op args[4]
  1.3 0.0 copy-start
  1.3 1.7 %copy-done = bf16[1536,768]{1,0:T(8,128)(2,1)S(1)} copy-done((bf16[1536,768]{1,0:T(8,128)(2,1)S(1)}, bf16[1536,768]{1,0:T(8,128)(2,1)}, u32[]{:S(2)}) %copy-start) | copy-done | bytes 2359320
  3.0 0.0 copy-start.1
  3.0 1.0 %copy-done.1 = bf16[256,768]{1,0:T(8,128)(2,1)S(1)} copy-done((bf16[256,768]{1,0:T(8,128)(2,1)S(1)}, bf16[256,768]{1,0:T(8,128)(2,1)}, u32[]{:S(2)}) %copy-start.1) | copy-done | bytes 393240
  4.0 0.0 copy-start.2
  4.0 0.7 %copy-done.2 = s32[192]{0:T(256)S(1)} copy-done((s32[192]{0:T(256)S(1)}, s32[192]{0:T(256)}, u32[]{:S(2)}) %copy-start.2) | copy-done | bytes 792
  4.7 0.0 copy-start.3
  4.7 0.7 %copy-done.3 = s32[32]{0:T(128)S(1)} copy-done((s32[32]{0:T(128)S(1)}, s32[32]{0:T(128)}, u32[]{:S(2)}) %copy-start.3) | copy-done | bytes 152
  5.3 44.2 %shard_map.68 = (f32[6,256]{1,0:T(8,128)S(1)}, f32[1,256]{1,0:T(1,128)S(1)}) custom-call(bf16[1536,768]{1,0:T(8,128)(2,1)S(1)} %copy-done, bf16[256,768]{1,0:T(8,128)(2,1)S(1)} %copy-done.1, s32[192]{0:T(256)S(1)} %copy-done.2, s32[32]{0:T(128)S(1)} %copy-done.3, s32[1,6,8]{2,1,0:T(8,128)S(1)} %copy.7.mask_ref), custom_call_target="tpu_custom_call" | custom-call | flops 4831838208 | bytes 5505024 | tf_op jit(solution)/shard_map/pallas_call | solution.py:254
  49.5 0.6 %reshape.10 = f32[1536]{0:T(1024)} reshape(f32[6,256]{1,0:T(8,128)S(1)} %get-tuple-element.4) | data formatting | bytes 12288 | tf_op jit(solution)/shard_map/reshape | solution.py:287
  50.1 0.6 %copy.9 = f32[256]{0:T(256)} copy(f32[256]{0:T(256)S(1)} %bitcast.1) | data formatting | bytes 2048
Async XLA Ops:
  1.3 1.7 %copy-start = (bf16[1536,768]{1,0:T(8,128)(2,1)S(1)}, bf16[1536,768]{1,0:T(8,128)(2,1)}, u32[]{:S(2)}) copy-start(bf16[1536,768]{1,0:T(8,128)(2,1)} %home_ref.1) | copy-start | bytes 7077892
  3.0 1.0 %copy-start.1 = (bf16[256,768]{1,0:T(8,128)(2,1)S(1)}, bf16[256,768]{1,0:T(8,128)(2,1)}, u32[]{:S(2)}) copy-start(bf16[256,768]{1,0:T(8,128)(2,1)} %guest_ref.1) | copy-start | bytes 1179652
  4.0 0.7 %copy-start.2 = (s32[192]{0:T(256)S(1)}, s32[192]{0:T(256)}, u32[]{:S(2)}) copy-start(s32[192]{0:T(256)} %home_ids.1) | copy-start | bytes 2308
  4.7 0.7 %copy-start.3 = (s32[32]{0:T(128)S(1)}, s32[32]{0:T(128)}, u32[]{:S(2)}) copy-start(s32[32]{0:T(128)} %guest_ids.1) | copy-start | bytes 388

commit v2 on v1

v2 whole, which is shorter than its diff:
```python
import functools

import jax
import jax.numpy as jnp
from jax import lax
from jax.experimental import pallas as pl
from jax.experimental.pallas import tpu as pltpu
from jax.sharding import PartitionSpec as P

BLOCK = 256
PARTS = 2
CHUNK = BLOCK // PARTS

SHARPNESS = 30.0
LOG2_E = 1.4426950408889634
EPSILON = 1e-06
MESH = pl.DeviceIdType.MESH


def lane_fold(value):
    return jnp.sum(value.reshape(value.shape[0] // 8, 8, value.shape[1]), axis=0)


def kernel(
    ndp, slots, home_ref, guest_ref, home_hbm, guest_hbm, mask_hbm, home_out, guest_out,
    rows, turned, blocks, inv_home, home_acc, col_parts, inbox, home_ids, guest_ids, mask,
    load_sem, own_sem, line_sem, side_sem, recv_sem, col_send, col_recv,
):
    d = lax.axis_index("dp")
    c = lax.axis_index("cluster")
    n_cluster = lax.axis_size("cluster")
    count = ndp // 2
    z = lax.div(d, 2)
    x = lax.rem(d, 2)
    mirror = c + 1 - 2 * lax.rem(c, 2)
    beside = d + 1 - 2 * x
    has_up = z < count - 1
    has_down = z > 0

    barrier = pltpu.get_barrier_semaphore()

    def greet(dp, cluster):
        pl.semaphore_signal(barrier, inc=1, device_id=(dp, cluster), device_id_type=MESH)

    greet(d, mirror)
    for column in (c, mirror):
        greet(beside, column)

        @pl.when(has_up)
        def _():
            greet(d + 2, column)

        @pl.when(has_down)
        def _():
            greet(d - 2, column)

    loads = [
        pltpu.make_async_copy(source, target, load_sem.at[i])
        for i, (source, target) in enumerate(
            ((home_ref, rows), (home_hbm, home_ids), (guest_hbm, guest_ids), (mask_hbm, mask))
        )
    ]
    for load in loads:
        load.start()

    pl.semaphore_wait(barrier, 3 + 2 * has_up.astype(jnp.int32) + 2 * has_down.astype(jnp.int32))

    def piece(part):
        return pl.ds(part * CHUNK, CHUNK)

    def own_copy(part, way, target):
        return pltpu.make_async_remote_copy(
            src_ref=guest_ref.at[piece(part), :],
            dst_ref=blocks.at[d, piece(part), :],
            send_sem=own_sem.at[way, part],
            recv_sem=recv_sem.at[d, part],
            device_id=(target, mirror),
            device_id_type=MESH,
        )

    def own_each(act):
        for part in range(PARTS):

            @pl.when(has_up)
            def _():
                act(own_copy(part, 0, d + 2))

            @pl.when(has_down)
            def _():
                act(own_copy(part, 1, d - 2))

            act(own_copy(part, 2, beside))
            act(own_copy(part, 3, d))

    own_each(lambda copy: copy.start())

    def passed(slot, part, sem, target):
        return pltpu.make_async_remote_copy(
            src_ref=blocks.at[slot, piece(part), :],
            dst_ref=blocks.at[slot, piece(part), :],
            send_sem=sem.at[slot, part],
            recv_sem=recv_sem.at[slot, part],
            device_id=(target, c),
            device_id_type=MESH,
        )

    def is_end(zz):
        return jnp.logical_or(zz == 0, zz == count - 1)

    def line_each(zz, part, act):
        slot = zz * 2 + x

        @pl.when(jnp.logical_and(has_up, zz < z))
        def _():
            act(passed(slot, part, line_sem, d + 2))

        @pl.when(jnp.logical_and(has_down, zz > z))
        def _():
            act(passed(slot, part, line_sem, d - 2))

        by_side = zz != z
        if part == PARTS - 1:
            by_side = jnp.logical_and(by_side, jnp.logical_not(is_end(zz)))

        @pl.when(by_side)
        def _():
            act(passed(slot, part, side_sem, beside))

    def end_each(zz, act):
        slot = zz * 2 + 1 - x

        @pl.when(jnp.logical_and(has_up, zz == 0))
        def _():
            act(passed(slot, PARTS - 1, line_sem, d + 2))

        @pl.when(jnp.logical_and(has_down, zz == count - 1))
        def _():
            act(passed(slot, PARTS - 1, line_sem, d - 2))

    def col_copy(slot):
        return pltpu.make_async_remote_copy(
            src_ref=col_parts.at[slot],
            dst_ref=inbox.at[d],
            send_sem=col_send.at[slot],
            recv_sem=col_recv.at[d],
            device_id=(slot, mirror),
            device_id_type=MESH,
        )

    for load in loads:
        load.wait()

    def prepare(slot, carry):
        own = rows[pl.ds(pl.multiple_of(slot * BLOCK, BLOCK), BLOCK), :]
        flipped = own.T
        turned[slot] = flipped
        values = flipped.astype(jnp.float32)
        total = jnp.sum(lane_fold(values * values), axis=0, keepdims=True)
        scale = (SHARPNESS * LOG2_E) / jnp.sqrt(total + EPSILON)
        inv_home[slot] = jnp.broadcast_to(scale, (8, BLOCK))
        home_acc[slot] = jnp.zeros((8, BLOCK), jnp.float32)
        return carry

    lax.fori_loop(0, slots, prepare, 0)

    def compute(slot):
        visitor = blocks[slot]
        values = visitor.astype(jnp.float32)
        inv = 1.0 / jnp.sqrt(jnp.sum(values * values, axis=1, keepdims=True) + EPSILON)
        guest_acc = jnp.zeros((BLOCK, 128), jnp.float32)
        for s in range(slots):
            products = jnp.dot(visitor, turned[s], preferred_element_type=jnp.float32)
            tile = jnp.exp2(products * inv * inv_home[s, 0:1, :])
            listed = mask[s, 0, slot].astype(jnp.float32)
            home_acc[s] += lane_fold(tile) * listed
            guest_acc += (tile[:, :128] + tile[:, 128:]) * listed
        col_parts[slot] = lane_fold(guest_acc.T)
        col_copy(slot).start()

    def both_ways(dist, act):
        def way(plus, carry):
            zz = z + (2 * plus - 1) * dist
            valid = (dist >= 0) & (zz >= 0) & (zz < count)
            valid = valid & jnp.logical_not((dist == 0) & (plus == 1))

            @pl.when(valid)
            def _():
                act(zz)

            return carry

        lax.fori_loop(0, 2, way, 0)

    def arrive(zz, xx, part):
        passed(zz * 2 + xx, part, line_sem, d).wait_recv()

    def line_part(part):
        def act(zz):
            arrive(zz, x, part)
            line_each(zz, part, lambda copy: copy.start())

        return act

    def end_part(zz):
        @pl.when(is_end(zz))
        def _():
            arrive(zz, 1 - x, PARTS - 1)
            end_each(zz, lambda copy: copy.start())

    def side_compute(zz):
        for part in range(PARTS - 1):
            arrive(zz, 1 - x, part)

        @pl.when(jnp.logical_not(is_end(zz)))
        def _():
            arrive(zz, 1 - x, PARTS - 1)

        compute(zz * 2 + 1 - x)

    def step(k, carry):
        for part in range(PARTS - 1):
            both_ways(k, line_part(part))
        both_ways(k - 2, side_compute)
        both_ways(k, line_part(PARTS - 1))
        both_ways(k, lambda zz: compute(zz * 2 + x))
        both_ways(k - 1, end_part)
        return carry

    lax.fori_loop(0, count + 2, step, 0)

    device = d * n_cluster + c
    home_list = home_ids[...]
    guest_list = guest_ids[...]

    def pick(ids, place):
        here = lax.broadcasted_iota(jnp.int32, ids.shape, 1) == place
        return jnp.sum(jnp.where(here, ids, 0), axis=1, keepdims=True)

    def log_members(own_id):
        number = jnp.sum((home_list == own_id).astype(jnp.int32), axis=1, keepdims=True)
        number += jnp.sum((guest_list == own_id).astype(jnp.int32), axis=1, keepdims=True)
        return jnp.log(number.astype(jnp.float32))

    for s in range(slots):
        density = jnp.sum(home_acc[s], axis=0, keepdims=True)
        score = jnp.log(1.0 + density) - log_members(pick(home_list, device * slots + s))
        home_out[:, s * BLOCK : (s + 1) * BLOCK] = score
    log_guest = log_members(pick(guest_list, device))

    own_each(lambda copy: copy.wait_send())

    def drain(t, carry):
        for part in range(PARTS):
            line_each(t, part, lambda copy: copy.wait_send())
        end_each(t, lambda copy: copy.wait_send())
        return carry

    lax.fori_loop(0, count, drain, 0)

    def collect(t, total):
        pltpu.make_async_remote_copy(
            src_ref=col_parts.at[t],
            dst_ref=inbox.at[t],
            send_sem=col_send.at[t],
            recv_sem=col_recv.at[t],
            device_id=(t, mirror),
            device_id_type=MESH,
        ).wait_recv()
        return total + inbox[t]

    total = lax.fori_loop(0, ndp, collect, jnp.zeros((8, BLOCK), jnp.float32))
    guest_out[...] = jnp.log(1.0 + jnp.sum(total, axis=0, keepdims=True)) - log_guest

    def col_drain(t, carry):
        col_copy(t).wait_send()
        return carry

    lax.fori_loop(0, ndp, col_drain, 0)


def body(home_rows, guest_rows, home_cluster, guest_cluster, pair_mask):
    slots = home_rows.shape[0] // BLOCK
    width = home_rows.shape[1]
    ndp = lax.axis_size("dp")
    hbm = pl.BlockSpec(memory_space=pltpu.HBM)
    vmem = pl.BlockSpec(memory_space=pltpu.VMEM)
    pairs = slots * ndp * BLOCK * BLOCK
    home_score, guest_score = pl.pallas_call(
        functools.partial(kernel, ndp, slots),
        out_shape=(
            jax.ShapeDtypeStruct((1, slots * BLOCK), jnp.float32),
            jax.ShapeDtypeStruct((1, BLOCK), jnp.float32),
        ),
        in_specs=[hbm] * 5,
        out_specs=(vmem, vmem),
        scratch_shapes=[
            pltpu.VMEM((slots * BLOCK, width), jnp.bfloat16),
            pltpu.VMEM((slots, width, BLOCK), jnp.bfloat16),
            pltpu.VMEM((ndp, BLOCK, width), jnp.bfloat16),
            pltpu.VMEM((slots, 8, BLOCK), jnp.float32),
            pltpu.VMEM((slots, 8, BLOCK), jnp.float32),
            pltpu.VMEM((ndp, 8, BLOCK), jnp.float32),
            pltpu.VMEM((ndp, 8, BLOCK), jnp.float32),
            pltpu.VMEM((1, home_cluster.shape[0]), jnp.int32),
            pltpu.VMEM((1, guest_cluster.shape[0]), jnp.int32),
            pltpu.SMEM((slots, 1, ndp), jnp.int32),
            pltpu.SemaphoreType.DMA((4,)),
            pltpu.SemaphoreType.DMA((4, PARTS)),
            pltpu.SemaphoreType.DMA((ndp, PARTS)),
            pltpu.SemaphoreType.DMA((ndp, PARTS)),
            pltpu.SemaphoreType.DMA((ndp, PARTS)),
            pltpu.SemaphoreType.DMA((ndp,)),
            pltpu.SemaphoreType.DMA((ndp,)),
        ],
        compiler_params=pltpu.CompilerParams(
            collective_id=0, has_side_effects=True, vmem_limit_bytes=64 * 2**20
        ),
        cost_estimate=pl.CostEstimate(
            flops=2 * pairs * width,
            bytes_accessed=2 * (home_rows.size + ndp * BLOCK * width),
            transcendentals=pairs,
        ),
    )(
        home_rows,
        guest_rows,
        home_cluster.reshape(1, -1),
        guest_cluster.reshape(1, -1),
        pair_mask.transpose(1, 0, 2),
    )
    return (home_score.reshape(-1), guest_score.reshape(-1))


def solution(mesh):
    placed = (
        P(("dp", "cluster"), None),
        P(("dp", "cluster"), None),
        P(),
        P(),
        P(("dp", "cluster"), None, None),
    )
    return jax.shard_map(
        body,
        mesh=mesh,
        in_specs=placed,
        out_specs=(P(("dp", "cluster")), P(("dp", "cluster"))),
        check_vma=False,
    )
```

time: 50.9 us -> 46.3 us (0.910)
  local copies, waits for them, and re-layouts: 5.84 us -> 1.22 us
  other arithmetic: 0 us -> 1.31 us
  Pallas kernels: 44.2 us -> 42.9 us
    unnamed x10 -> x1, local copies, waits for them, and re-layouts: 5.24 us -> 1.22 us
    pallas_call x0 -> x1, other arithmetic: none -> 1.31 us  [body(): pl.pallas_call(functools.partial(kernel, ndp, slots), out_shape=(jax.Shap...]
    pallas_call x1, Pallas kernels: 44.2 us -> 42.9 us  [body(): pl.pallas_call(functools.partial(kernel, ndp, slots), out_shape=(jax.Shap...]
    reshape x1 -> x0, local copies, waits for them, and re-layouts: 0.6 us -> none  [body(): return (home_score.reshape(-1), guest_score.reshape(-1))]
where the time goes in v2:
time: 46.3 us; the launch traced here: 46.1 us
  Pallas kernels  42.9 us (93%)
  other arithmetic  1.31 us (3%)
  local copies, waits for them, and re-layouts  1.22 us (3%)
  between operations  0.64 us (1%)
    pallas_call x1, Pallas kernels, body(): pl.pallas_call(functools.partial(kernel, ndp, slots), out_shape=(jax.Shap...  42.9 us
    pallas_call x1, other arithmetic, body(): pl.pallas_call(functools.partial(kernel, ndp, slots), out_shape=(jax.Shap...  1.31 us
    unnamed x1, local copies, waits for them, and re-layouts  1.22 us

profile of v2, /device:TPU:1, one launch (start us, length us, event | category | flops | bytes accessed | tf_op | source)
XLA Modules:
  0.0 46.1 jit_solution(17644731687699169510)
XLA Ops:
  0.6 42.9 %shard_map.68 = (f32[1,1536]{1,0:T(1,128)}, f32[1,256]{1,0:T(1,128)}) custom-call(bf16[1536,768]{1,0:T(8,128)(2,1)} %home_ref.1, bf16[256,768]{1,0:T(8,128)(2,1)} %guest_ref.1, s32[1,192]{1,0:T(1,128)} %bitcast.6, s32[1,32]{1,0:T(1,128)} %bitcast.7, s32[6,1,8]{2,1,0:T(1,128)} %bitcast.5), custom_call_target="tpu_custom_call" | custom-call | flops 4831838208 | bytes 5505024 | tf_op jit(solution)/shard_map/pallas_call | solution.py:288
  43.5 1.3 %reduce = f32[1536]{0:T(1024)} reduce(f32[1,1536]{1,0:T(1,128)} %get-tuple-element.4, f32[]{:T(128)} %constant.1), dimensions={0}, to_apply=%get-tuple-element.4.reduce_sub_computation | reduce | bytes 12292 | tf_op jit(solution)/shard_map/pallas_call | solution.py:288
  44.8 1.2 %copy.8 = f32[256]{0:T(256)} copy(f32[256]{0:T(256)} %bitcast.4) | data formatting | bytes 2048

commit v3 on v2

--- a/solution.py
+++ b/solution.py
@@ -8,7 +8,7 @@
 from jax.sharding import PartitionSpec as P
 
 BLOCK = 256
-PARTS = 2
+PARTS = 4
 CHUNK = BLOCK // PARTS
 
 SHARPNESS = 30.0
@@ -78,8 +78,8 @@
             device_id_type=MESH,
         )
 
-    def own_each(act):
-        for part in range(PARTS):
+    def own_each(act, parts):
+        for part in parts:
 
             @pl.when(has_up)
             def _():
@@ -92,7 +92,7 @@
             act(own_copy(part, 2, beside))
             act(own_copy(part, 3, d))
 
-    own_each(lambda copy: copy.start())
+    own_each(lambda copy: copy.start(), range(PARTS // 2))
 
     def passed(slot, part, sem, target):
         return pltpu.make_async_remote_copy(
@@ -119,23 +119,23 @@
             act(passed(slot, part, line_sem, d - 2))
 
         by_side = zz != z
-        if part == PARTS - 1:
+        if part >= PARTS // 2:
             by_side = jnp.logical_and(by_side, jnp.logical_not(is_end(zz)))
 
         @pl.when(by_side)
         def _():
             act(passed(slot, part, side_sem, beside))
 
-    def end_each(zz, act):
+    def end_each(zz, part, act):
         slot = zz * 2 + 1 - x
 
         @pl.when(jnp.logical_and(has_up, zz == 0))
         def _():
-            act(passed(slot, PARTS - 1, line_sem, d + 2))
+            act(passed(slot, part, line_sem, d + 2))
 
         @pl.when(jnp.logical_and(has_down, zz == count - 1))
         def _():
-            act(passed(slot, PARTS - 1, line_sem, d - 2))
+            act(passed(slot, part, line_sem, d - 2))
 
     def col_copy(slot):
         return pltpu.make_async_remote_copy(
@@ -161,7 +161,13 @@
         home_acc[slot] = jnp.zeros((8, BLOCK), jnp.float32)
         return carry
 
-    lax.fori_loop(0, slots, prepare, 0)
+    later = range(PARTS // 2, PARTS)
+    done = 0
+    for i, part in enumerate(later):
+        upto = slots * (i + 1) // len(later)
+        lax.fori_loop(done, upto, prepare, 0)
+        done = upto
+        own_each(lambda copy: copy.start(), (part,))
 
     def compute(slot):
         visitor = blocks[slot]
@@ -201,29 +207,32 @@
 
         return act
 
-    def end_part(zz):
+    def end_parts(zz):
         @pl.when(is_end(zz))
         def _():
-            arrive(zz, 1 - x, PARTS - 1)
-            end_each(zz, lambda copy: copy.start())
+            for part in range(PARTS // 2, PARTS):
+                arrive(zz, 1 - x, part)
+                end_each(zz, part, lambda copy: copy.start())
 
     def side_compute(zz):
-        for part in range(PARTS - 1):
+        for part in range(PARTS // 2):
             arrive(zz, 1 - x, part)
 
         @pl.when(jnp.logical_not(is_end(zz)))
         def _():
-            arrive(zz, 1 - x, PARTS - 1)
+            for part in range(PARTS // 2, PARTS):
+                arrive(zz, 1 - x, part)
 
         compute(zz * 2 + 1 - x)
 
     def step(k, carry):
-        for part in range(PARTS - 1):
+        for part in range(PARTS // 2):
             both_ways(k, line_part(part))
         both_ways(k - 2, side_compute)
-        both_ways(k, line_part(PARTS - 1))
+        for part in range(PARTS // 2, PARTS):
+            both_ways(k, line_part(part))
         both_ways(k, lambda zz: compute(zz * 2 + x))
-        both_ways(k - 1, end_part)
+        both_ways(k - 1, end_parts)
         return carry
 
     lax.fori_loop(0, count + 2, step, 0)
@@ -247,12 +256,13 @@
         home_out[:, s * BLOCK : (s + 1) * BLOCK] = score
     log_guest = log_members(pick(guest_list, device))
 
-    own_each(lambda copy: copy.wait_send())
+    own_each(lambda copy: copy.wait_send(), range(PARTS))
 
     def drain(t, carry):
         for part in range(PARTS):
             line_each(t, part, lambda copy: copy.wait_send())
-        end_each(t, lambda copy: copy.wait_send())
+        for part in range(PARTS // 2, PARTS):
+            end_each(t, part, lambda copy: copy.wait_send())
         return carry
 
     lax.fori_loop(0, count, drain, 0)
@@ -288,8 +298,8 @@
     home_score, guest_score = pl.pallas_call(
         functools.partial(kernel, ndp, slots),
         out_shape=(
-            jax.ShapeDtypeStruct((1, slots * BLOCK), jnp.float32),
-            jax.ShapeDtypeStruct((1, BLOCK), jnp.float32),
+            pltpu.VMEM((1, slots * BLOCK), jnp.float32),
+            pltpu.VMEM((1, BLOCK), jnp.float32),
         ),
         in_specs=[hbm] * 5,
         out_specs=(vmem, vmem),
@@ -313,7 +323,7 @@
             pltpu.SemaphoreType.DMA((ndp,)),
         ],
         compiler_params=pltpu.CompilerParams(
-            collective_id=0, has_side_effects=True, vmem_limit_bytes=64 * 2**20
+            collective_id=0, has_side_effects=True, vmem_limit_bytes=62 * 2**20
         ),
         cost_estimate=pl.CostEstimate(
             flops=2 * pairs * width,

time: 46.3 us -> 44.8 us (0.968)
  other arithmetic: 1.31 us -> 0.62 us
  local copies, waits for them, and re-layouts: 1.22 us -> 0.56 us
    pallas_call x1, other arithmetic: 1.31 us -> 0.62 us  [body(): pl.pallas_call(functools.partial(kernel, ndp, slots), out_shape=(pltpu.VM...]
    unnamed x1, local copies, waits for them, and re-layouts: 1.22 us -> 0.56 us
where the time goes in v3:
time: 44.8 us; the launch traced here: 44.6 us
  Pallas kernels  42.8 us (96%)
  between operations  0.64 us (1%)
  other arithmetic  0.62 us (1%)
  local copies, waits for them, and re-layouts  0.56 us (1%)
    pallas_call x1, Pallas kernels, body(): pl.pallas_call(functools.partial(kernel, ndp, slots), out_shape=(pltpu.VM...  42.8 us

profile of v3, /device:TPU:1, one launch (start us, length us, event | category | flops | bytes accessed | tf_op | source)
XLA Modules:
  0.0 44.6 jit_solution(14857815649074362765)
XLA Ops:
  0.6 42.8 %shard_map.68 = (f32[1,1536]{1,0:T(1,128)S(1)}, f32[1,256]{1,0:T(1,128)S(1)}) custom-call(bf16[1536,768]{1,0:T(8,128)(2,1)} %home_ref.1, bf16[256,768]{1,0:T(8,128)(2,1)} %guest_ref.1, s32[1,192]{1,0:T(1,128)} %bitcast.6, s32[1,32]{1,0:T(1,128)} %bitcast.7, s32[6,1,8]{2,1,0:T(1,128)} %bitcast.5), custom_call_target="tpu_custom_call" | custom-call | flops 4831838208 | bytes 5505024 | tf_op jit(solution)/shard_map/pallas_call | solution.py:298
  43.4 0.6 %copy.8 = f32[256]{0:T(256)} copy(f32[256]{0:T(256)S(1)} %bitcast.4) | data formatting | bytes 2048
  44.0 0.6 %reduce = f32[1536]{0:T(1024)} reduce(f32[1,1536]{1,0:T(1,128)S(1)} %get-tuple-element.4, f32[]{:T(128)} %constant.1), dimensions={0}, to_apply=%get-tuple-element.4.reduce_sub_computation | reduce | bytes 12292 | tf_op jit(solution)/shard_map/pallas_call | solution.py:298

commit v4 on v3

--- a/solution.py
+++ b/solution.py
@@ -12,7 +12,6 @@
 CHUNK = BLOCK // PARTS
 
 SHARPNESS = 30.0
-LOG2_E = 1.4426950408889634
 EPSILON = 1e-06
 MESH = pl.DeviceIdType.MESH
 
@@ -156,7 +155,7 @@
         turned[slot] = flipped
         values = flipped.astype(jnp.float32)
         total = jnp.sum(lane_fold(values * values), axis=0, keepdims=True)
-        scale = (SHARPNESS * LOG2_E) / jnp.sqrt(total + EPSILON)
+        scale = SHARPNESS / jnp.sqrt(total + EPSILON)
         inv_home[slot] = jnp.broadcast_to(scale, (8, BLOCK))
         home_acc[slot] = jnp.zeros((8, BLOCK), jnp.float32)
         return carry
@@ -169,18 +168,25 @@
         done = upto
         own_each(lambda copy: copy.start(), (part,))
 
-    def compute(slot):
-        visitor = blocks[slot]
+    def compute(slot, first, extent):
+        visitor = blocks[slot, first : first + extent, :]
         values = visitor.astype(jnp.float32)
         inv = 1.0 / jnp.sqrt(jnp.sum(values * values, axis=1, keepdims=True) + EPSILON)
-        guest_acc = jnp.zeros((BLOCK, 128), jnp.float32)
+        inv = jnp.broadcast_to(inv, (extent, 128))
+        guest_acc = jnp.zeros((extent, 128), jnp.float32)
         for s in range(slots):
             products = jnp.dot(visitor, turned[s], preferred_element_type=jnp.float32)
-            tile = jnp.exp2(products * inv * inv_home[s, 0:1, :])
             listed = mask[s, 0, slot].astype(jnp.float32)
-            home_acc[s] += lane_fold(tile) * listed
-            guest_acc += (tile[:, :128] + tile[:, 128:]) * listed
-        col_parts[slot] = lane_fold(guest_acc.T)
+            both = jnp.zeros((extent, 128), jnp.float32)
+            for lanes in (slice(0, 128), slice(128, 256)):
+                tile = jnp.exp(products[:, lanes] * inv * inv_home[s, 0:1, lanes])
+                home_acc[s, :, lanes] += lane_fold(tile) * listed
+                both += tile
+            guest_acc += both * listed
+        col_parts[slot, :, first : first + extent] = lane_fold(guest_acc.T)
+
+    def compute_all(slot):
+        compute(slot, 0, BLOCK)
         col_copy(slot).start()
 
     def both_ways(dist, act):
@@ -223,7 +229,7 @@
             for part in range(PARTS // 2, PARTS):
                 arrive(zz, 1 - x, part)
 
-        compute(zz * 2 + 1 - x)
+        compute_all(zz * 2 + 1 - x)
 
     def step(k, carry):
         for part in range(PARTS // 2):
@@ -231,11 +237,22 @@
         both_ways(k - 2, side_compute)
         for part in range(PARTS // 2, PARTS):
             both_ways(k, line_part(part))
-        both_ways(k, lambda zz: compute(zz * 2 + x))
+        both_ways(k, lambda zz: compute_all(zz * 2 + x))
         both_ways(k - 1, end_parts)
         return carry
 
-    lax.fori_loop(0, count + 2, step, 0)
+    lax.fori_loop(0, count, step, 0)
+    both_ways(count - 2, side_compute)
+
+    def far_compute(zz):
+        slot = zz * 2 + 1 - x
+        for half in range(2):
+            for part in range(half * PARTS // 2, (half + 1) * PARTS // 2):
+                arrive(zz, 1 - x, part)
+            compute(slot, half * BLOCK // 2, BLOCK // 2)
+        col_copy(slot).start()
+
+    both_ways(count - 1, far_compute)
 
     device = d * n_cluster + c
     home_list = home_ids[...]

time: 44.8 us -> 44.7 us (level)
  no operation moved by 1% of the time
where the time goes in v4:
time: 44.7 us; the launch traced here: 44.6 us
  Pallas kernels  42.7 us (96%)
  between operations  0.64 us (1%)
  other arithmetic  0.62 us (1%)
  local copies, waits for them, and re-layouts  0.56 us (1%)
    pallas_call x1, Pallas kernels, body(): pl.pallas_call(functools.partial(kernel, ndp, slots), out_shape=(pltpu.VM...  42.7 us

profile of v4, /device:TPU:1, one launch (start us, length us, event | category | flops | bytes accessed | tf_op | source)
XLA Modules:
  0.0 44.6 jit_solution(11269643649680219491)
XLA Ops:
  0.6 42.7 %shard_map.68 = (f32[1,1536]{1,0:T(1,128)S(1)}, f32[1,256]{1,0:T(1,128)S(1)}) custom-call(bf16[1536,768]{1,0:T(8,128)(2,1)} %home_ref.1, bf16[256,768]{1,0:T(8,128)(2,1)} %guest_ref.1, s32[1,192]{1,0:T(1,128)} %bitcast.6, s32[1,32]{1,0:T(1,128)} %bitcast.7, s32[6,1,8]{2,1,0:T(1,128)} %bitcast.5), custom_call_target="tpu_custom_call" | custom-call | flops 4831838208 | bytes 5505024 | tf_op jit(solution)/shard_map/pallas_call | solution.py:315
  43.4 0.6 %copy.8 = f32[256]{0:T(256)} copy(f32[256]{0:T(256)S(1)} %bitcast.4) | data formatting | bytes 2048
  43.9 0.6 %reduce = f32[1536]{0:T(1024)} reduce(f32[1,1536]{1,0:T(1,128)S(1)} %get-tuple-element.4, f32[]{:T(128)} %constant.1), dimensions={0}, to_apply=%get-tuple-element.4.reduce_sub_computation | reduce | bytes 12292 | tf_op jit(solution)/shard_map/pallas_call | solution.py:315

commit v5 on v4

--- a/solution.py
+++ b/solution.py
@@ -232,13 +232,12 @@
         compute_all(zz * 2 + 1 - x)
 
     def step(k, carry):
-        for part in range(PARTS // 2):
+        both_ways(jnp.where(k > 1, k - 1, -1), end_parts)
+        both_ways(k - 2, side_compute)
+        for part in range(PARTS):
             both_ways(k, line_part(part))
-        both_ways(k - 2, side_compute)
-        for part in range(PARTS // 2, PARTS):
-            both_ways(k, line_part(part))
+        both_ways(jnp.where(k == 1, 0, -1), end_parts)
         both_ways(k, lambda zz: compute_all(zz * 2 + x))
-        both_ways(k - 1, end_parts)
         return carry
 
     lax.fori_loop(0, count, step, 0)

time: 44.7 us -> 45.1 us (level)
  no operation moved by 1% of the time
where the time goes in v5:
time: 45.1 us; the launch traced here: 44.9 us
  Pallas kernels  43.1 us (96%)
  between operations  0.64 us (1%)
  other arithmetic  0.62 us (1%)
  local copies, waits for them, and re-layouts  0.56 us (1%)
    pallas_call x1, Pallas kernels, body(): pl.pallas_call(functools.partial(kernel, ndp, slots), out_shape=(pltpu.VM...  43.1 us

profile of v5, /device:TPU:1, one launch (start us, length us, event | category | flops | bytes accessed | tf_op | source)
XLA Modules:
  0.0 44.9 jit_solution(12142814848522873507)
XLA Ops:
  0.6 43.1 %shard_map.68 = (f32[1,1536]{1,0:T(1,128)S(1)}, f32[1,256]{1,0:T(1,128)S(1)}) custom-call(bf16[1536,768]{1,0:T(8,128)(2,1)} %home_ref.1, bf16[256,768]{1,0:T(8,128)(2,1)} %guest_ref.1, s32[1,192]{1,0:T(1,128)} %bitcast.6, s32[1,32]{1,0:T(1,128)} %bitcast.7, s32[6,1,8]{2,1,0:T(1,128)} %bitcast.5), custom_call_target="tpu_custom_call" | custom-call | flops 4831838208 | bytes 5505024 | tf_op jit(solution)/shard_map/pallas_call | solution.py:314
  43.7 0.6 %copy.8 = f32[256]{0:T(256)} copy(f32[256]{0:T(256)S(1)} %bitcast.4) | data formatting | bytes 2048
  44.3 0.6 %reduce = f32[1536]{0:T(1024)} reduce(f32[1,1536]{1,0:T(1,128)S(1)} %get-tuple-element.4, f32[]{:T(128)} %constant.1), dimensions={0}, to_apply=%get-tuple-element.4.reduce_sub_computation | reduce | bytes 12292 | tf_op jit(solution)/shard_map/pallas_call | solution.py:314

commit v6 on v4

--- a/solution.py
+++ b/solution.py
@@ -10,6 +10,7 @@
 BLOCK = 256
 PARTS = 4
 CHUNK = BLOCK // PARTS
+BY_SIDE = PARTS
 
 SHARPNESS = 30.0
 EPSILON = 1e-06
@@ -118,7 +119,7 @@
             act(passed(slot, part, line_sem, d - 2))
 
         by_side = zz != z
-        if part >= PARTS // 2:
+        if part >= BY_SIDE:
             by_side = jnp.logical_and(by_side, jnp.logical_not(is_end(zz)))
 
         @pl.when(by_side)
@@ -155,7 +156,7 @@
         turned[slot] = flipped
         values = flipped.astype(jnp.float32)
         total = jnp.sum(lane_fold(values * values), axis=0, keepdims=True)
-        scale = SHARPNESS / jnp.sqrt(total + EPSILON)
+        scale = SHARPNESS * lax.rsqrt(total + EPSILON)
         inv_home[slot] = jnp.broadcast_to(scale, (8, BLOCK))
         home_acc[slot] = jnp.zeros((8, BLOCK), jnp.float32)
         return carry
@@ -171,7 +172,7 @@
     def compute(slot, first, extent):
         visitor = blocks[slot, first : first + extent, :]
         values = visitor.astype(jnp.float32)
-        inv = 1.0 / jnp.sqrt(jnp.sum(values * values, axis=1, keepdims=True) + EPSILON)
+        inv = lax.rsqrt(jnp.sum(values * values, axis=1, keepdims=True) + EPSILON)
         inv = jnp.broadcast_to(inv, (extent, 128))
         guest_acc = jnp.zeros((extent, 128), jnp.float32)
         for s in range(slots):
@@ -216,17 +217,17 @@
     def end_parts(zz):
         @pl.when(is_end(zz))
         def _():
-            for part in range(PARTS // 2, PARTS):
+            for part in range(BY_SIDE, PARTS):
                 arrive(zz, 1 - x, part)
                 end_each(zz, part, lambda copy: copy.start())
 
     def side_compute(zz):
-        for part in range(PARTS // 2):
+        for part in range(BY_SIDE):
             arrive(zz, 1 - x, part)
 
         @pl.when(jnp.logical_not(is_end(zz)))
         def _():
-            for part in range(PARTS // 2, PARTS):
+            for part in range(BY_SIDE, PARTS):
                 arrive(zz, 1 - x, part)
 
         compute_all(zz * 2 + 1 - x)
@@ -278,7 +279,7 @@
     def drain(t, carry):
         for part in range(PARTS):
             line_each(t, part, lambda copy: copy.wait_send())
-        for part in range(PARTS // 2, PARTS):
+        for part in range(BY_SIDE, PARTS):
             end_each(t, part, lambda copy: copy.wait_send())
         return carry
 

time: 44.7 us -> 48.1 us (1.076)
  Pallas kernels: 42.7 us -> 46.2 us
    pallas_call x1, Pallas kernels: 42.7 us -> 46.2 us  [body(): pl.pallas_call(functools.partial(kernel, ndp, slots), out_shape=(pltpu.VM...]
where the time goes in v6:
time: 48.1 us; the launch traced here: 48 us
  Pallas kernels  46.2 us (96%)
  between operations  0.64 us (1%)
  other arithmetic  0.62 us (1%)
  local copies, waits for them, and re-layouts  0.56 us (1%)
    pallas_call x1, Pallas kernels, body(): pl.pallas_call(functools.partial(kernel, ndp, slots), out_shape=(pltpu.VM...  46.2 us

profile of v6, /device:TPU:1, one launch (start us, length us, event | category | flops | bytes accessed | tf_op | source)
XLA Modules:
  0.0 48.0 jit_solution(13453373660361124562)
XLA Ops:
  0.6 46.2 %shard_map.68 = (f32[1,1536]{1,0:T(1,128)S(1)}, f32[1,256]{1,0:T(1,128)S(1)}) custom-call(bf16[1536,768]{1,0:T(8,128)(2,1)} %home_ref.1, bf16[256,768]{1,0:T(8,128)(2,1)} %guest_ref.1, s32[1,192]{1,0:T(1,128)} %bitcast.6, s32[1,32]{1,0:T(1,128)} %bitcast.7, s32[6,1,8]{2,1,0:T(1,128)} %bitcast.5), custom_call_target="tpu_custom_call" | custom-call | flops 4831838208 | bytes 5505024 | tf_op jit(solution)/shard_map/pallas_call | solution.py:316
  46.8 0.6 %copy.8 = f32[256]{0:T(256)} copy(f32[256]{0:T(256)S(1)} %bitcast.4) | data formatting | bytes 2048
  47.4 0.6 %reduce = f32[1536]{0:T(1024)} reduce(f32[1,1536]{1,0:T(1,128)S(1)} %get-tuple-element.4, f32[]{:T(128)} %constant.1), dimensions={0}, to_apply=%get-tuple-element.4.reduce_sub_computation | reduce | bytes 12292 | tf_op jit(solution)/shard_map/pallas_call | solution.py:316

commit v7 on v6

--- a/solution.py
+++ b/solution.py
@@ -10,7 +10,7 @@
 BLOCK = 256
 PARTS = 4
 CHUNK = BLOCK // PARTS
-BY_SIDE = PARTS
+BY_SIDE = 1
 
 SHARPNESS = 30.0
 EPSILON = 1e-06
@@ -243,6 +243,22 @@
         return carry
 
     lax.fori_loop(0, count, step, 0)
+    device = d * n_cluster + c
+    home_list = home_ids[...]
+    guest_list = guest_ids[...]
+
+    def pick(ids, place):
+        here = lax.broadcasted_iota(jnp.int32, ids.shape, 1) == place
+        return jnp.sum(jnp.where(here, ids, 0), axis=1, keepdims=True)
+
+    def log_members(own_id):
+        number = jnp.sum((home_list == own_id).astype(jnp.int32), axis=1, keepdims=True)
+        number += jnp.sum((guest_list == own_id).astype(jnp.int32), axis=1, keepdims=True)
+        return jnp.log(number.astype(jnp.float32))
+
+    log_home = [log_members(pick(home_list, device * slots + s)) for s in range(slots)]
+    log_guest = log_members(pick(guest_list, device))
+
     both_ways(count - 2, side_compute)
 
     def far_compute(zz):
@@ -255,24 +271,10 @@
 
     both_ways(count - 1, far_compute)
 
-    device = d * n_cluster + c
-    home_list = home_ids[...]
-    guest_list = guest_ids[...]
-
-    def pick(ids, place):
-        here = lax.broadcasted_iota(jnp.int32, ids.shape, 1) == place
-        return jnp.sum(jnp.where(here, ids, 0), axis=1, keepdims=True)
-
-    def log_members(own_id):
-        number = jnp.sum((home_list == own_id).astype(jnp.int32), axis=1, keepdims=True)
-        number += jnp.sum((guest_list == own_id).astype(jnp.int32), axis=1, keepdims=True)
-        return jnp.log(number.astype(jnp.float32))
-
     for s in range(slots):
         density = jnp.sum(home_acc[s], axis=0, keepdims=True)
-        score = jnp.log(1.0 + density) - log_members(pick(home_list, device * slots + s))
+        score = jnp.log(1.0 + density) - log_home[s]
         home_out[:, s * BLOCK : (s + 1) * BLOCK] = score
-    log_guest = log_members(pick(guest_list, device))
 
     own_each(lambda copy: copy.wait_send(), range(PARTS))
 

time: 48.1 us -> 46.5 us (0.967)
  Pallas kernels: 46.2 us -> 44.6 us
    pallas_call x1, Pallas kernels: 46.2 us -> 44.6 us  [body(): pl.pallas_call(functools.partial(kernel, ndp, slots), out_shape=(pltpu.VM...]
where the time goes in v7:
time: 46.5 us; the launch traced here: 46.4 us
  Pallas kernels  44.6 us (96%)
  between operations  0.64 us (1%)
  other arithmetic  0.62 us (1%)
  local copies, waits for them, and re-layouts  0.56 us (1%)
    pallas_call x1, Pallas kernels, body(): pl.pallas_call(functools.partial(kernel, ndp, slots), out_shape=(pltpu.VM...  44.6 us

profile of v7, /device:TPU:1, one launch (start us, length us, event | category | flops | bytes accessed | tf_op | source)
XLA Modules:
  0.0 46.4 jit_solution(423491218055412540)
XLA Ops:
  0.6 44.6 %shard_map.68 = (f32[1,1536]{1,0:T(1,128)S(1)}, f32[1,256]{1,0:T(1,128)S(1)}) custom-call(bf16[1536,768]{1,0:T(8,128)(2,1)} %home_ref.1, bf16[256,768]{1,0:T(8,128)(2,1)} %guest_ref.1, s32[1,192]{1,0:T(1,128)} %bitcast.6, s32[1,32]{1,0:T(1,128)} %bitcast.7, s32[6,1,8]{2,1,0:T(1,128)} %bitcast.5), custom_call_target="tpu_custom_call" | custom-call | flops 4831838208 | bytes 5505024 | tf_op jit(solution)/shard_map/pallas_call | solution.py:318
  45.2 0.6 %copy.8 = f32[256]{0:T(256)} copy(f32[256]{0:T(256)S(1)} %bitcast.4) | data formatting | bytes 2048
  45.8 0.6 %reduce = f32[1536]{0:T(1024)} reduce(f32[1,1536]{1,0:T(1,128)S(1)} %get-tuple-element.4, f32[]{:T(128)} %constant.1), dimensions={0}, to_apply=%get-tuple-element.4.reduce_sub_computation | reduce | bytes 12292 | tf_op jit(solution)/shard_map/pallas_call | solution.py:318

commit v8 on v7

--- a/solution.py
+++ b/solution.py
@@ -10,7 +10,7 @@
 BLOCK = 256
 PARTS = 4
 CHUNK = BLOCK // PARTS
-BY_SIDE = 1
+BY_SIDE = PARTS // 2
 
 SHARPNESS = 30.0
 EPSILON = 1e-06
@@ -161,13 +161,9 @@
         home_acc[slot] = jnp.zeros((8, BLOCK), jnp.float32)
         return carry
 
-    later = range(PARTS // 2, PARTS)
-    done = 0
-    for i, part in enumerate(later):
-        upto = slots * (i + 1) // len(later)
-        lax.fori_loop(done, upto, prepare, 0)
-        done = upto
-        own_each(lambda copy: copy.start(), (part,))
+    lax.fori_loop(0, slots // 2, prepare, 0)
+    own_each(lambda copy: copy.start(), range(PARTS // 2, PARTS))
+    lax.fori_loop(slots // 2, slots, prepare, 0)
 
     def compute(slot, first, extent):
         visitor = blocks[slot, first : first + extent, :]
@@ -234,15 +230,22 @@
 
     def step(k, carry):
         for part in range(PARTS // 2):
-            both_ways(k, line_part(part))
+            both_ways(jnp.where(k > 1, k, -1), line_part(part))
+        both_ways(jnp.where(k > 1, k - 1, -1), end_parts)
         both_ways(k - 2, side_compute)
         for part in range(PARTS // 2, PARTS):
             both_ways(k, line_part(part))
+        both_ways(jnp.where(k == 1, 0, -1), end_parts)
         both_ways(k, lambda zz: compute_all(zz * 2 + x))
-        both_ways(k - 1, end_parts)
         return carry
 
-    lax.fori_loop(0, count, step, 0)
+    for part in range(PARTS // 2):
+        both_ways(1, line_part(part))
+    for part in range(PARTS):
+        arrive(z, x, part)
+    compute_all(d)
+    lax.fori_loop(1, count, step, 0)
+
     device = d * n_cluster + c
     home_list = home_ids[...]
     guest_list = guest_ids[...]

time: 46.5 us -> 44.6 us (0.959)
  Pallas kernels: 44.6 us -> 42.6 us
    pallas_call x1, Pallas kernels: 44.6 us -> 42.6 us  [body(): pl.pallas_call(functools.partial(kernel, ndp, slots), out_shape=(pltpu.VM...]
where the time goes in v8:
time: 44.6 us; the launch traced here: 44.5 us
  Pallas kernels  42.6 us (96%)
  between operations  0.64 us (1%)
  other arithmetic  0.62 us (1%)
  local copies, waits for them, and re-layouts  0.56 us (1%)
    pallas_call x1, Pallas kernels, body(): pl.pallas_call(functools.partial(kernel, ndp, slots), out_shape=(pltpu.VM...  42.6 us

profile of v8, /device:TPU:1, one launch (start us, length us, event | category | flops | bytes accessed | tf_op | source)
XLA Modules:
  0.0 44.5 jit_solution(18372206808596654231)
XLA Ops:
  0.6 42.6 %shard_map.68 = (f32[1,1536]{1,0:T(1,128)S(1)}, f32[1,256]{1,0:T(1,128)S(1)}) custom-call(bf16[1536,768]{1,0:T(8,128)(2,1)} %home_ref.1, bf16[256,768]{1,0:T(8,128)(2,1)} %guest_ref.1, s32[1,192]{1,0:T(1,128)} %bitcast.6, s32[1,32]{1,0:T(1,128)} %bitcast.7, s32[6,1,8]{2,1,0:T(1,128)} %bitcast.5), custom_call_target="tpu_custom_call" | custom-call | flops 4831838208 | bytes 5505024 | tf_op jit(solution)/shard_map/pallas_call | solution.py:321
  43.3 0.6 %copy.8 = f32[256]{0:T(256)} copy(f32[256]{0:T(256)S(1)} %bitcast.4) | data formatting | bytes 2048
  43.8 0.6 %reduce = f32[1536]{0:T(1024)} reduce(f32[1,1536]{1,0:T(1,128)S(1)} %get-tuple-element.4, f32[]{:T(128)} %constant.1), dimensions={0}, to_apply=%get-tuple-element.4.reduce_sub_computation | reduce | bytes 12292 | tf_op jit(solution)/shard_map/pallas_call | solution.py:321
